TPU v7x, 512 devices: a whole 4x8x8 slice. The times are simulated.
512 devices in a mesh: rows: 64 (over x, y, core), probe: 8 (over z).
Axes of the slice: x: 4, y: 8, z: 8, core: 2. Of those that a mesh axis runs over, the one named last changes fastest.
Arguments:
- targets: float32 [3, 65536], P(None, 'rows'), may hold values from 0 to 1
- sources: bfloat16 [3, 8192], P(None, 'rows'), may hold values from 0 to 1
- probes: bfloat16 [256, 8192], P('probe', 'rows'), may hold values from -6 to 6
- cluster_sizes: int32 [512], P(('rows', 'probe')), may hold values from 64 to 128, as said below
- leaf_ranks: int32 [512], P(('rows', 'probe')), may hold values from 128 to 256, as said below
Outputs:
- leaf_basis: float32 [256, 2, 65536], P(None, None, ('rows', 'probe'))
- top_factor: float32 [512, 256, 256], P(('rows', 'probe'))
Inputs may be any that keep to these rules, and one draw needn't show every extreme that they name: `cluster_sizes`: some leaf uses all 128 points in every draw. `leaf_ranks`: some leaf keeps all 256 rows in every draw.
All inputs are finite; a program needn't handle non-finite values.
Results may differ from a plain program's by a relative error of at most 0.0033.
Values may be sent and summed in bfloat16 or wider, within the bound.
A program may use at most 64 MiB of HBM per device.

v0:
```python
import math

import jax
import jax.numpy as jnp
from jax import lax
from jax.sharding import PartitionSpec as P

wavenumber = 30.0
softening = 0.02


def partner_2(value, axis, apart):
    mask = 2**apart
    pairs = [(source, source ^ mask) for source in range(lax.axis_size(axis))]
    return lax.ppermute(value, axis, pairs)


def kernel_pair(source_pts, target_pts, col_total):
    diff_x = source_pts[0][:, None] - target_pts[0][None, :]
    diff_y = source_pts[1][:, None] - target_pts[1][None, :]
    diff_z = source_pts[2][:, None] - target_pts[2][None, :]
    distance = jnp.sqrt(diff_x * diff_x + diff_y * diff_y + diff_z * diff_z + softening * softening)
    amplitude = 1.0 / (distance * jnp.sqrt(jnp.float32(col_total)))
    kernel_cos = (amplitude * jnp.cos(wavenumber * distance)).astype(jnp.bfloat16)
    kernel_sin = (amplitude * jnp.sin(wavenumber * distance)).astype(jnp.bfloat16)
    return (kernel_cos, kernel_sin)


def sample_block(probe_piece, source_piece, target_pts, col_total):
    columns = probe_piece.shape[1]
    block_cols = math.gcd(columns, 256)
    block_count = columns // block_cols
    probe_parts = probe_piece.reshape(probe_piece.shape[0], block_count, block_cols).transpose(
        1, 0, 2
    )
    source_parts = source_piece.reshape(3, block_count, block_cols).transpose(1, 0, 2)

    def advance(running, pieces):
        probe_part, source_part = pieces
        kernel_cos, kernel_sin = kernel_pair(source_part.astype(jnp.float32), target_pts, col_total)
        part_cos = jnp.dot(probe_part, kernel_cos, preferred_element_type=jnp.float32)
        part_sin = jnp.dot(probe_part, kernel_sin, preferred_element_type=jnp.float32)
        return (running + jnp.stack([part_cos, part_sin]), None)

    starting = jnp.zeros((2, probe_piece.shape[0], target_pts.shape[1]), jnp.float32)
    result, _ = lax.scan(advance, starting, (probe_parts, source_parts))
    return result


def make_adder(target_pts, col_total):

    def add_columns(running, pieces, offset_col):
        return sample_block(pieces[0], pieces[1], target_pts, col_total)

    return add_columns


def cholesky_basis(matrix, nprobe_total):
    gram_matrix = jnp.dot(matrix, matrix.T, precision=lax.Precision.HIGHEST)
    shift_value = jnp.trace(gram_matrix) / nprobe_total
    factor = jnp.linalg.cholesky(
        gram_matrix + shift_value * jnp.eye(nprobe_total, dtype=matrix.dtype)
    )
    return jax.scipy.linalg.solve_triangular(factor, matrix, lower=True)


def per_device(targets, sources, probes, cluster_sizes, leaf_ranks):
    col_total = sources.shape[1] * lax.axis_size("rows")
    nprobe_total = probes.shape[0] * lax.axis_size("probe")
    leaf_rows = targets.shape[1] // lax.axis_size("probe")
    own_targets = lax.dynamic_slice_in_dim(
        targets, lax.axis_index("probe") * leaf_rows, leaf_rows, 1
    )
    all_probes = lax.all_gather(probes, "probe", axis=0, tiled=True)
    adder = make_adder(own_targets, col_total)
    starting = jnp.zeros((2, nprobe_total, leaf_rows), jnp.float32)
    samples = adder(
        starting,
        (
            lax.all_gather(all_probes, "rows", axis=1, tiled=True),
            lax.all_gather(sources, "rows", axis=1, tiled=True),
        ),
        jnp.int32(0),
    )
    kept_rows = (jnp.arange(leaf_rows) < cluster_sizes[0]).astype(jnp.float32)
    matrix = jnp.concatenate([samples[0] * kept_rows, samples[1] * kept_rows], axis=1)
    basis_rows = cholesky_basis(matrix, nprobe_total)
    rank_rows = (jnp.arange(nprobe_total) < leaf_ranks[0]).astype(jnp.float32)
    basis_rows = basis_rows * rank_rows[:, None]
    projected = jnp.dot(matrix, basis_rows.T, precision=lax.Precision.HIGHEST)
    row_index = lax.axis_index("rows")
    for tree_bit in range(2):
        partner = partner_2(projected, "rows", tree_bit)
        is_left = row_index >> tree_bit & 1 == 0
        left_part = jnp.where(is_left, projected, partner)
        right_part = jnp.where(is_left, partner, projected)
        stacked = jnp.concatenate([left_part, right_part], axis=1)
        node_basis = cholesky_basis(stacked, nprobe_total)
        projected = jnp.dot(stacked, node_basis.T, precision=lax.Precision.HIGHEST)
    return (basis_rows.reshape(nprobe_total, 2, leaf_rows), projected[None])


def solution(mesh):
    return jax.shard_map(
        per_device,
        mesh=mesh,
        in_specs=(
            P(None, "rows"),
            P(None, "rows"),
            P("probe", "rows"),
            P(("rows", "probe")),
            P(("rows", "probe")),
        ),
        out_specs=(P(None, None, ("rows", "probe")), P(("rows", "probe"), None, None)),
        check_vma=False,
    )
```

profile of v0, /device:TPU:1, one launch (start us, length us, event | category | flops | bytes accessed | tf_op | source)
XLA Modules:
  0.0 452.6 jit_solution(17370533172197070458)
XLA Ops:
  7.2 25.9 %all_gather.9 = bf16[256,128]{1,0:T(8,128)(2,1)S(1)} all-gather(bf16[32,128]{1,0:T(8,128)(2,1)} %param.12), channel_id=1, replica_groups=mesh['rows'=64,'probe'=8] {'probe'}, dimensions={0}, use_global_device_ids=true | all-gather | bytes 73728 | tf_op jit(solution)/shard_map/all_gather | solution.py:74
  35.2 46.2 %all_gather.11 = bf16[3,8192]{1,0:T(4,128)(2,1)S(1)} all-gather(bf16[3,128]{1,0:T(4,128)(2,1)} %param.11), channel_id=1, replica_groups=mesh['rows'=64,'probe'=8] {'rows'}, dimensions={1}, use_global_device_ids=true | all-gather | bytes 49920 | tf_op jit(solution)/shard_map/all_gather | solution.py:81
  81.4 41.8 %all-gather.2.cloned.1.call-done = bf16[256,8192]{0,1:T(8,128)(2,1)} async-done(((bf16[256,128]{0,1:T(8,128)(2,1)}), bf16[256,8192]{0,1:T(8,128)(2,1)}) %all-gather.2.cloned.1.call-update) | async-done | bytes 4194320 | tf_op jit(solution)/shard_map/all_gather | solution.py:80
  123.2 113.8 %while.17 = (s32[]{:T(128)}, f32[2,256,128]{2,1,0:T(8,128)S(1)}, bf16[32,256,256]{1,2,0:T(8,128)(2,1)}, bf16[32,3,256]{2,1,0:T(4,128)(2,1)S(1)}, f32[3,128]{1,0:T(4,128)S(1)}, /*index=5*/s32[]{:T(128)}, s32[]{:T(128)}) while((s32[]{:T(128)}, f32[2,256,128]{2,1,0:T(8,128)S(1)}, bf16[32,256,256]{1,2,0:T(8,128)(2,1)}, ...), condition=%wide.region_1.2_spmd.clone, body=%wide.region_0.1_spmd.clone.sunk | while | flops 34669312 | bytes 1334875 | solution.py:46
  124.9 1.7 convolution_bitcast_fusion.5
  128.5 1.7 convolution_bitcast_fusion.5
  132.0 1.7 convolution_bitcast_fusion.5
  135.6 1.7 convolution_bitcast_fusion.5
  139.1 1.7 convolution_bitcast_fusion.5
  142.6 1.7 convolution_bitcast_fusion.5
  149.7 1.7 convolution_bitcast_fusion.5
  153.3 1.7 convolution_bitcast_fusion.5
  160.3 1.7 convolution_bitcast_fusion.5
  163.9 1.7 convolution_bitcast_fusion.5
  171.0 1.7 convolution_bitcast_fusion.5
  174.5 1.7 convolution_bitcast_fusion.5
  178.1 1.7 convolution_bitcast_fusion.5
  181.6 1.7 convolution_bitcast_fusion.5
  185.1 1.7 convolution_bitcast_fusion.5
  192.2 1.7 convolution_bitcast_fusion.5
  195.8 1.7 convolution_bitcast_fusion.5
  202.9 1.7 convolution_bitcast_fusion.5
  206.4 1.7 convolution_bitcast_fusion.5
  213.5 1.7 convolution_bitcast_fusion.5
  217.0 1.7 convolution_bitcast_fusion.5
  224.1 1.7 convolution_bitcast_fusion.5
  227.7 1.7 convolution_bitcast_fusion.5
  231.2 1.7 convolution_bitcast_fusion.5
  234.7 1.7 convolution_bitcast_fusion.5
  239.0 11.7 %cholesky.172 = f32[128,128]{1,0:T(8,128)S(1)} custom-call(f32[128,128]{1,0:T(8,128)S(1)} %cholesky.270), custom_call_target="Cholesky" | custom-call | tf_op jit(solution)/shard_map/jit(cholesky)/cholesky | solution.py:61
  250.7 9.8 %custom-call.20 = f32[1,128,128]{1,2,0:T(8,128)S(1)} custom-call(f32[1,128,128]{2,1,0:T(8,128)S(1)} %get-tuple-element.157), custom_call_target="InvertDiagBlocksLowerTriangular" | custom-call | tf_op jit(solution)/shard_map/jit(cholesky)/cholesky | solution.py:61
  261.0 11.7 %cholesky.189 = f32[128,128]{1,0:T(8,128)S(1)} custom-call(f32[128,128]{1,0:T(8,128)S(1)} %convolution_subtract_fusion.3), custom_call_target="Cholesky" | custom-call | tf_op jit(solution)/shard_map/jit(cholesky)/cholesky | solution.py:61
  275.2 4.2 while.16
  279.5 19.8 %custom-call.15 = f32[2,128,128]{1,2,0:T(8,128)S(1)} custom-call(f32[2,128,128]{2,1,0:T(8,128)S(1)} %get-tuple-element.47), custom_call_target="InvertDiagBlocksLowerTriangular" | custom-call | tf_op jit(solution)/shard_map/jit(_solve_triangular)/triangular_solve | solution.py:64
  300.7 2.2 collective-permute-start
  306.7 11.7 %cholesky.206 = f32[128,128]{1,0:T(8,128)S(1)} custom-call(f32[128,128]{1,0:T(8,128)S(1)} %cholesky.273), custom_call_target="Cholesky" | custom-call | tf_op jit(solution)/shard_map/jit(cholesky)/cholesky | solution.py:61
  318.4 9.8 %custom-call.21 = f32[1,128,128]{1,2,0:T(8,128)S(1)} custom-call(f32[1,128,128]{2,1,0:T(8,128)S(1)} %get-tuple-element.155), custom_call_target="InvertDiagBlocksLowerTriangular" | custom-call | tf_op jit(solution)/shard_map/jit(cholesky)/cholesky | solution.py:61
  328.7 11.7 %cholesky.223 = f32[128,128]{1,0:T(8,128)S(1)} custom-call(f32[128,128]{1,0:T(8,128)S(1)} %convolution_subtract_fusion.2), custom_call_target="Cholesky" | custom-call | tf_op jit(solution)/shard_map/jit(cholesky)/cholesky | solution.py:61
  343.2 4.3 while.18
  347.6 19.7 %custom-call.22 = f32[2,128,128]{1,2,0:T(8,128)S(1)} custom-call(f32[2,128,128]{2,1,0:T(8,128)S(1)} %get-tuple-element.72), custom_call_target="InvertDiagBlocksLowerTriangular" | custom-call | tf_op jit(solution)/shard_map/jit(_solve_triangular)/triangular_solve | solution.py:64
  369.4 2.0 collective-permute-start.1
  372.6 6.3 %collective-permute-done.1 = f32[256,256]{0,1:T(8,128)S(1)} collective-permute-done((f32[256,256]{0,1:T(8,128)S(1)}, f32[256,256]{0,1:T(8,128)S(1)}, u32[]{:S(2)}, u32[]{:S(2)}) %collective-permute-start.1) | collective-permute-done | bytes 262176 | tf_op jit(solution)/shard_map/ppermute | solution.py:15
  381.5 11.7 %cholesky.240 = f32[128,128]{1,0:T(8,128)S(1)} custom-call(f32[128,128]{1,0:T(8,128)S(1)} %cholesky.276), custom_call_target="Cholesky" | custom-call | tf_op jit(solution)/shard_map/jit(cholesky)/cholesky | solution.py:61
  393.2 9.8 %custom-call.23 = f32[1,128,128]{1,2,0:T(8,128)S(1)} custom-call(f32[1,128,128]{2,1,0:T(8,128)S(1)} %get-tuple-element.151), custom_call_target="InvertDiagBlocksLowerTriangular" | custom-call | tf_op jit(solution)/shard_map/jit(cholesky)/cholesky | solution.py:61
  403.5 11.7 %cholesky.257 = f32[128,128]{1,0:T(8,128)S(1)} custom-call(f32[128,128]{1,0:T(8,128)S(1)} %convolution_subtract_fusion.1), custom_call_target="Cholesky" | custom-call | tf_op jit(solution)/shard_map/jit(cholesky)/cholesky | solution.py:61
  418.0 4.4 while.19
  422.4 19.7 %custom-call.24 = f32[2,128,128]{1,2,0:T(8,128)S(1)} custom-call(f32[2,128,128]{2,1,0:T(8,128)S(1)} %get-tuple-element.73), custom_call_target="InvertDiagBlocksLowerTriangular" | custom-call | tf_op jit(solution)/shard_map/jit(_solve_triangular)/triangular_solve | solution.py:64
  443.6 1.7 convolution_bitcast_fusion.2
  (264 shorter events, 99.8 us)
Async XLA Ops:
  7.2 74.2 %copy-start = (f32[3,1024]{1,0:T(4,128)S(1)}, f32[3,1024]{1,0:T(4,128)}, u32[]{:S(2)}) copy-start(f32[3,1024]{1,0:T(4,128)} %param.10) | copy-start | bytes 36868
  7.2 116.0 %all-gather.2.cloned.1.call-start = ((), (), s32[]{:S(2)}) async-start(), calls=%async_computation | async-start | bytes 4259840 | tf_op jit(solution)/shard_map/all_gather | solution.py:80
  300.7 3.4 collective-permute-start
  369.4 9.6 %collective-permute-start.1 = (f32[256,256]{0,1:T(8,128)S(1)}, f32[256,256]{0,1:T(8,128)S(1)}, u32[]{:S(2)}, u32[]{:S(2)}) collective-permute-start(f32[256,256]{0,1:T(8,128)S(1)} %fusion.30), channel_id=1, source_target_pairs={{0,16},{8,24},{16,0},{24,8},{32,48},{40,56},{48,32},{56,40},{64,80... | collective-permute-start | bytes 786440 | tf_op jit(solution)/shard_map/ppermute | solution.py:15
Sparse Core Ops, SparseCore 0:
  34.0 89.1 all-gather.1
where the time goes:
time: 457 us; the launch traced here: 453 us
  other arithmetic  167 us (37%)
  matrix products  121 us (26%)
  blocking collectives  72.1 us (16%)
  waiting for transfers between devices  49.3 us (11%)
  between operations  22.2 us (5%)
  local copies, waits for them, and re-layouts  14.3 us (3%)
    another operation x20, other arithmetic, cholesky_basis(): jnp.linalg.cholesky(gram_matrix + shift_value * jnp.eye(nprobe_total, dty...  103 us
    another operation x7, other arithmetic, cholesky_basis(): return jax.scipy.linalg.solve_triangular(factor, matrix, lower=True)  59.3 us
    dot_general x32, matrix products, advance(): jnp.dot(probe_part, kernel_sin, preferred_element_type=jnp.float32)  54.3 us
    dot_general x32, matrix products, advance(): jnp.dot(probe_part, kernel_cos, preferred_element_type=jnp.float32)  54.1 us
    all_gather x1, blocking collectives, per_device(): lax.all_gather(sources, 'rows', axis=1, tiled=True)  46.2 us
    all_gather x1, waiting for transfers between devices, per_device(): lax.all_gather(all_probes, 'rows', axis=1, tiled=True)  41.8 us
    all_gather x1, blocking collectives, per_device(): all_probes = lax.all_gather(probes, 'probe', axis=0, tiled=True)  25.9 us
  transfers between devices with their start and end apart: 3, of which 3 were waited for; matrix products, arithmetic and copies ran while one was open for 0% of the time, Pallas kernels for 0%

commit v1 on v0

v1 whole, which is shorter than its diff:
```python
import functools
import math

import jax
import jax.numpy as jnp
from jax import lax
from jax.experimental import pallas as pl
from jax.experimental.pallas import tpu as pltpu
from jax.sharding import PartitionSpec as P

MESH = pl.DeviceIdType.MESH
BF = jnp.bfloat16
F32 = jnp.float32
WAVENUMBER = 30.0
SOFTENING = 0.02
NX, NY, NZ, NC = 4, 8, 8, 2
GROUPS = (2, 1, 3, 0)
RING = (4, 3, 5, 2, 6, 1, 7)
HALF = 16
LEAF = 128
NPROBE = 256
SPREAD = NPROBE + 2.0
SIN_TERMS = (3.1415926401839527, -5.167710090327096, 2.5500776596356878, -0.5982921588728, 0.07765940703413433)
COS_TERMS = (0.999999953466513, -4.934792858655427, 4.058411913769729, -1.3318801587034552, 0.2196967935096479)
NN = (((1,), (0,)), ((), ()))
NT = (((1,), (1,)), ((), ()))
TN = (((0,), (0,)), ((), ()))


def horner(terms, value, factor):
    total = terms[-1] * factor
    for term in terms[-2::-1]:
        total = total * value + term * factor
    return total


def sample_kernel(
    col_total, targets_ref, sources_ref, probes_ref, out_ref,
    tgt, src, spread, part_a, part_b, lhs, kmat, pair_out, own, pair_in, line_out, line_in,
    send_sem, recv_sem,
):
    r, z = lax.axis_index("rows"), lax.axis_index("probe")
    x, y, c = r // (NY * NC), (r // NC) % NY, r % NC

    def at(xx, yy, cc):
        return (xx * NY + yy) * NC + cc

    y_peer = {d: (at(x, lax.rem(y + d, NY), c), z) for d in range(1, NY)}
    z_peer = {d: (r, lax.rem(z + d, NZ)) for d in range(1, NZ)}
    xc_peer = {
        (dx, dc): (at(lax.rem(x + dx, NX), y, lax.rem(c + dc, NC)), z)
        for dx in range(NX) for dc in range(NC) if (dx, dc) != (0, 0)
    }
    peers = list(y_peer.values()) + list(z_peer.values()) + list(xc_peer.values())
    barrier = pltpu.get_barrier_semaphore()
    for peer in peers:
        pl.semaphore_signal(barrier, inc=1, device_id=peer, device_id_type=MESH)

    scale = WAVENUMBER / (2.0 * math.pi)
    pad = jnp.zeros((5, LEAF), F32)
    own_cols = pl.ds(pl.multiple_of(z * LEAF, LEAF), LEAF)
    tgt[x * NC + c] = jnp.concatenate([targets_ref[:, own_cols] * scale, pad], axis=0)
    src[y] = jnp.concatenate([sources_ref[...].astype(F32) * scale, pad], axis=0)
    part_a[y, z] = probes_ref[0:HALF, :]
    part_b[z, y] = probes_ref[HALF : 2 * HALF, :]
    pl.semaphore_wait(barrier, len(peers))

    slots = iter(range(64))

    def send(from_ref, to_ref, peer):
        slot = next(slots)
        copy = pltpu.make_async_remote_copy(
            src_ref=from_ref, dst_ref=to_ref, send_sem=send_sem.at[slot], recv_sem=recv_sem.at[slot],
            device_id=peer, device_id_type=MESH,
        )
        copy.start()
        return copy

    order = RING
    src_copies = [send(src.at[y], src.at[y], y_peer[d]) for d in order]
    tgt_copies = [send(tgt.at[x * NC + c], tgt.at[x * NC + c], peer) for peer in xc_peer.values()]
    a_copies = [send(part_a.at[y, z], part_a.at[y, z], z_peer[d]) for d in order]
    b_copies = [send(part_b.at[z, y], part_b.at[z, y], y_peer[d]) for d in order]

    for copy in src_copies:
        copy.wait_recv()
    for yy in range(NY):
        for axis in range(3):
            row = src[yy, axis : axis + 1, :]
            spread[axis, yy * LEAF : (yy + 1) * LEAF, :] = jnp.broadcast_to(row, (LEAF, LEAF)).T
    for copy in a_copies:
        copy.wait_recv()
    a2_copies = [send(part_a.at[y], part_a.at[y], y_peer[d]) for d in order]
    for copy in b_copies:
        copy.wait_recv()
    b2_copies = [send(part_b.at[z], part_b.at[z], z_peer[d]) for d in order]
    for copy in tgt_copies:
        copy.wait_recv()

    amp = scale / math.sqrt(col_total)
    root = math.sqrt(2.0 * amp)
    soft = (SOFTENING * scale) ** 2
    chunk = 64

    def fill(group):
        xx = lax.rem(x + GROUPS[group], NX)
        leaf = [tgt[xx * NC + lax.rem(c + 1, NC)], tgt[xx * NC + c]]

        def body(i, carry):
            rows = pl.ds(pl.multiple_of(i * chunk, chunk), chunk)
            for role in range(2):
                dx = spread[0, rows, :] - leaf[role][0:1, :]
                dy = spread[1, rows, :] - leaf[role][1:2, :]
                dz = spread[2, rows, :] - leaf[role][2:3, :]
                squared = (dx * dx + dy * dy) + (dz * dz + soft)
                inverse = lax.rsqrt(squared)
                turns = squared * inverse
                turns = turns - jnp.round(turns)
                t2 = turns * turns
                sine = turns * horner(SIN_TERMS, t2, root)
                cosine = horner(COS_TERMS, t2, root)
                lead = inverse * sine
                base = role * 2 * LEAF
                kmat[group, rows, base : base + LEAF] = (amp * inverse - lead * sine).astype(BF)
                kmat[group, rows, base + LEAF : base + 2 * LEAF] = (lead * cosine).astype(BF)
            return carry

        lax.fori_loop(0, NY * LEAF // chunk, body, 0)

    def multiply(group):
        part = jnp.dot(lhs[...], kmat[group], preferred_element_type=F32)
        pair_out[group] = part[:, : 2 * LEAF]
        own[group] = part[:, 2 * LEAF :]
        return send(pair_out.at[group], pair_in.at[group], xc_peer[(0, 1)])

    for group in range(len(GROUPS)):
        fill(group)
    for copy in a2_copies + b2_copies:
        copy.wait_recv()
    for yy in range(NY):
        cols = slice(yy * LEAF, (yy + 1) * LEAF)
        lhs[: NPROBE // 2, cols] = part_a[yy].reshape(NPROBE // 2, LEAF)
        lhs[NPROBE // 2 :, cols] = part_b[:, yy].reshape(NPROBE // 2, LEAF)
    pair_copies, line_copies = [], []

    def pass_on(group):
        pair_copies[group].wait_recv()
        line_out[group] = (own[group] + pair_in[group]).astype(line_out.dtype)
        line_copies.append(send(line_out.at[group], line_in.at[group], xc_peer[(GROUPS[group], 0)]))

    for group in range(len(GROUPS)):
        pair_copies.append(multiply(group))
        if group >= 1:
            pass_on(group - 1)
    pair_copies[3].wait_recv()
    total = own[3] + pair_in[3]
    for group in range(3):
        line_copies[group].wait_recv()
        total = total + line_in[group].astype(F32)
    for half in range(2):
        for zz in range(NZ):
            to, frm = (2 * zz + half) * HALF, (half * NZ + zz) * HALF
            out_ref[to : to + HALF, :] = total[frm : frm + HALF, :]
    for copy in src_copies + tgt_copies + a_copies + b_copies + a2_copies + b2_copies + pair_copies + line_copies:
        copy.wait_send()


def split(a):
    high = a.astype(BF)
    return high, (a - high.astype(F32)).astype(BF)


def mm(a, b, dims):
    return lax.dot_general(a, b, dims, preferred_element_type=F32)


def dot_split(a, b, dims=NN):
    (ah, al), (bh, bl) = a, b
    return mm(ah, bh, dims) + (mm(ah, bl, dims) + mm(al, bh, dims))


def dot3(a, b, dims=NN):
    return dot_split(split(a), split(b), dims)


def diagonal(n):
    return lax.broadcasted_iota(jnp.int32, (n, n), 0) == lax.broadcasted_iota(jnp.int32, (n, n), 1)


def eye(n):
    return diagonal(n).astype(F32)


def spd_inverses(mats, low):
    alpha = 2.0 / (1.0 + SPREAD)
    delta = (SPREAD - 1.0) / (SPREAD + 1.0)
    inv_low = 1.0 / low
    ids = [eye(m.shape[0]) for m in mats]
    rest = [i - (alpha * inv_low) * m for i, m in zip(ids, mats)]
    found = None
    while True:
        c = 2.0 / (2.0 - delta * delta)
        delta = delta * delta / (2.0 - delta * delta)
        parts = [split(v) for v in rest]
        if found is None:
            found = [(c * alpha) * (i + v) for i, v in zip(ids, rest)]
        else:
            found = [c * (f + dot_split(split(f), p)) for f, p in zip(found, parts)]
        if delta < 1e-5:
            return [f * inv_low for f in found]
        rest = [(1.0 - c) * i + c * dot_split(p, p) for i, p in zip(ids, parts)]


def lanes(tile, k):
    return jnp.broadcast_to(tile[:, k : k + 1], tile.shape)


def base_inverse(blocks, in_ref, out_ref, panel=8):
    n = blocks[0].shape[0]
    for b, block in enumerate(blocks):
        in_ref[:, b, :] = jnp.concatenate([block, eye(n)], axis=1)
    v = [in_ref[k] for k in range(n)]
    for k in range(0, n, panel):
        p = [[lanes(v[k + i], k + j) for j in range(i + 1)] for i in range(panel)]
        low = [[None] * panel for _ in range(panel)]
        r, x, u = [None] * panel, [None] * panel, [None] * panel
        for j in range(panel):
            r[j] = lax.rsqrt(p[j][j])
            x[j] = v[k + j] * r[j]
            out_ref[k + j] = x[j]
            for i in range(j + 1, panel):
                low[i][j] = p[i][j] * r[j]
            for i in range(j + 1, panel):
                for m in range(j + 1, i + 1):
                    p[i][m] = p[i][m] - low[i][j] * low[m][j]
                v[k + i] = v[k + i] - low[i][j] * x[j]
        for j in reversed(range(panel)):
            u[j] = x[j] * r[j]
            for m in range(j):
                x[m] = x[m] - low[j][m] * u[j]
        for i in range(k + panel, n):
            t = [lanes(v[i], k + j) * u[j] for j in range(panel)]
            while len(t) > 1:
                t = [a + b for a, b in zip(t[::2], t[1::2])]
            v[i] = v[i] - t[0]


BASE = 32
LINE = F32


def chol_inverse(h, low, in_ref, out_ref):
    level, stack = [h], []
    while level[0].shape[0] > BASE:
        m = level[0].shape[0] // 2
        a11 = [b[:m, :m] for b in level]
        a21 = [b[m:, :m] for b in level]
        inverses = spd_inverses(a11, low)
        w = [dot3(p, q) for p, q in zip(a21, inverses)]
        schur = [b[m:, m:] - dot3(q, p, NT) for b, q, p in zip(level, w, a21)]
        stack.append(w)
        level = [b for pair in zip(a11, schur) for b in pair]
    base_inverse(level, in_ref, out_ref)
    xs = [out_ref[:, i, :][:, BASE:] for i in range(len(level))]
    while stack:
        joined = []
        for i, w in enumerate(stack.pop()):
            first, second = xs[2 * i], xs[2 * i + 1]
            top = jnp.concatenate([first, jnp.zeros_like(first)], axis=1)
            joined.append(jnp.concatenate([top, jnp.concatenate([-dot3(second, w), second], axis=1)], axis=0))
        xs = joined
    return xs[0]


def shift_of(gram):
    kept = jnp.where(diagonal(NPROBE), gram, 0.0)
    return jnp.sum(jnp.sum(kept, axis=0, keepdims=True), axis=1, keepdims=True) * (1.0 / NPROBE)


def leaf_kernel(size_ref, rank_ref, samples_ref, basis_ref, gram_ref, in_ref, out_ref):
    col = lax.broadcasted_iota(jnp.int32, (NPROBE, 2 * LEAF), 1) % LEAF
    matrix = split(jnp.where(col < size_ref[0], samples_ref[...], 0.0))
    gram = dot_split(matrix, matrix, NT)
    shift = shift_of(gram)
    inverse = chol_inverse(gram + shift * eye(NPROBE), shift, in_ref, out_ref)
    row = lax.broadcasted_iota(jnp.int32, (NPROBE, NPROBE), 0)
    inverse = split(jnp.where(row < rank_ref[0], inverse, 0.0))
    projected = split(dot_split(inverse, split(gram)))
    gram_ref[...] = dot_split(projected, projected, TN)
    basis = dot_split(inverse, matrix)
    basis_ref[:, 0, :] = basis[:, :LEAF]
    basis_ref[:, 1, :] = basis[:, LEAF:]


def middle_kernel(left_ref, right_ref, gram_ref):
    gram = left_ref[...] + right_ref[...]
    shift = shift_of(gram)
    inverse = spd_inverses([gram + shift * eye(NPROBE)], shift)[0]
    gram_ref[...] = gram - shift * eye(NPROBE) + (shift * shift) * inverse


def top_kernel(left_ref, right_ref, top_ref, in_ref, out_ref):
    gram = left_ref[...] + right_ref[...]
    shift = shift_of(gram)
    inverse = chol_inverse(gram + shift * eye(NPROBE), shift, in_ref, out_ref)
    top_ref[0] = dot3(gram, inverse, NT)


def per_device(targets, sources, probes, cluster_sizes, leaf_ranks):
    col_total = sources.shape[1] * lax.axis_size("rows")
    square = jax.ShapeDtypeStruct((NPROBE, NPROBE), F32)
    vmem = pl.BlockSpec(memory_space=pltpu.VMEM)
    smem = pl.BlockSpec(memory_space=pltpu.SMEM)
    base = [pltpu.VMEM((BASE, 8, 2 * BASE), F32)] * 2
    samples = pl.pallas_call(
        functools.partial(sample_kernel, col_total),
        out_shape=square,
        in_specs=[vmem] * 3,
        out_specs=vmem,
        scratch_shapes=[
            pltpu.VMEM((NX * NC, 8, LEAF), F32),
            pltpu.VMEM((NY, 8, LEAF), F32),
            pltpu.VMEM((3, NY * LEAF, LEAF), F32),
            pltpu.VMEM((NY, NZ, HALF, LEAF), BF),
            pltpu.VMEM((NZ, NY, HALF, LEAF), BF),
            pltpu.VMEM((NPROBE, NY * LEAF), BF),
            pltpu.VMEM((4, NY * LEAF, 4 * LEAF), BF),
            pltpu.VMEM((4, NPROBE, 2 * LEAF), F32),
            pltpu.VMEM((4, NPROBE, 2 * LEAF), F32),
            pltpu.VMEM((4, NPROBE, 2 * LEAF), F32),
            pltpu.VMEM((3, NPROBE, 2 * LEAF), LINE),
            pltpu.VMEM((3, NPROBE, 2 * LEAF), LINE),
            pltpu.SemaphoreType.DMA((49,)),
            pltpu.SemaphoreType.DMA((49,)),
        ],
        compiler_params=pltpu.CompilerParams(
            collective_id=0, has_side_effects=True, vmem_limit_bytes=40 * 1024 * 1024
        ),
    )(targets, sources, probes)
    small = pltpu.CompilerParams(vmem_limit_bytes=40 * 1024 * 1024)
    basis, gram = pl.pallas_call(
        leaf_kernel,
        out_shape=(jax.ShapeDtypeStruct((NPROBE, 2, LEAF), F32), square),
        in_specs=[smem, smem, vmem],
        out_specs=(vmem, vmem),
        scratch_shapes=base,
        compiler_params=small,
    )(cluster_sizes, leaf_ranks, samples)
    pairs = [[(s, s ^ bit) for s in range(lax.axis_size("rows"))] for bit in (1, 2)]
    gram = pl.pallas_call(
        middle_kernel, out_shape=square, in_specs=[vmem] * 2, out_specs=vmem, compiler_params=small
    )(gram, lax.ppermute(gram, "rows", pairs[0]))
    top = pl.pallas_call(
        top_kernel,
        out_shape=jax.ShapeDtypeStruct((1, NPROBE, NPROBE), F32),
        in_specs=[vmem] * 2,
        out_specs=vmem,
        scratch_shapes=base,
        compiler_params=small,
    )(gram, lax.ppermute(gram, "rows", pairs[1]))
    return basis, top


def solution(mesh):
    return jax.shard_map(
        per_device,
        mesh=mesh,
        in_specs=(
            P(None, "rows"),
            P(None, "rows"),
            P("probe", "rows"),
            P(("rows", "probe")),
            P(("rows", "probe")),
        ),
        out_specs=(P(None, None, ("rows", "probe")), P(("rows", "probe"), None, None)),
        check_vma=False,
    )
```

time: 457 us -> 78.9 us (0.17)
  other arithmetic: 167 us -> 0 us
  matrix products: 121 us -> 0 us
  blocking collectives: 72.1 us -> 0 us
  Pallas kernels: 0 us -> 62.3 us
  waiting for transfers between devices: 49.3 us -> 8 us
  between operations: 22.2 us -> 1.99 us
  local copies, waits for them, and re-layouts: 14.3 us -> 1.42 us
    another operation x27 -> x0, other arithmetic: 163 us -> none  [the longest x20 103 us: cholesky_basis(): jnp.linalg.cholesky(gram_matrix + shift_value * jnp.eye(nprobe_total, dty...]
    dot_general x70 -> x0, matrix products: 115 us -> none  [the longest x32 54.3 us: advance(): jnp.dot(probe_part, kernel_sin, preferred_element_type=jnp.float32)]
    all_gather x2 -> x0, blocking collectives: 72.1 us -> none  [the longest x1 46.2 us: per_device(): lax.all_gather(sources, 'rows', axis=1, tiled=True)]
    pallas_call x0 -> x4, Pallas kernels: none -> 62.3 us  [the longest x1 43.8 us: per_device(): pl.pallas_call(functools.partial(sample_kernel, col_total), out_shape=squ...]
    all_gather x1 -> x0, waiting for transfers between devices: 41.8 us -> none  [per_device(): lax.all_gather(all_probes, 'rows', axis=1, tiled=True)]
    another operation x36 -> x0, local copies, waits for them, and re-layouts: 12.8 us -> none  [the longest x15 8.32 us: cholesky_basis(): return jax.scipy.linalg.solve_triangular(factor, matrix, lower=True)]
    another operation x15 -> x0, matrix products: 5.23 us -> none  [the longest x9 3.81 us: cholesky_basis(): return jax.scipy.linalg.solve_triangular(factor, matrix, lower=True)]
  transfers between devices with their start and end apart: 3 -> 2, of which waited for: 3 -> 2; matrix products, arithmetic and copies ran while one was open for 0% -> 0% of each run, Pallas kernels for 0% -> 0%
where the time goes in v1:
time: 78.9 us; the launch traced here: 78.5 us
  Pallas kernels  62.3 us (79%)
  waiting for transfers between devices  8 us (10%)
  starting transfers between devices  4.82 us (6%)
  between operations  1.99 us (3%)
  local copies, waits for them, and re-layouts  1.42 us (2%)
    pallas_call x1, Pallas kernels, per_device(): pl.pallas_call(functools.partial(sample_kernel, col_total), out_shape=squ...  43.8 us
    pallas_call x1, Pallas kernels, per_device(): pl.pallas_call(leaf_kernel, out_shape=(jax.ShapeDtypeStruct((NPROBE, 2, L...  8.25 us
    pallas_call x1, Pallas kernels, per_device(): pl.pallas_call(top_kernel, out_shape=jax.ShapeDtypeStruct((1, NPROBE, NPR...  7.63 us
    ppermute x1, waiting for transfers between devices, per_device(): lax.ppermute(gram, 'rows', pairs[1])  6.86 us
    pallas_call x1, Pallas kernels, per_device(): pl.pallas_call(middle_kernel, out_shape=square, in_specs=[vmem] * 2, out_...  2.57 us
    ppermute x1, starting transfers between devices, per_device(): lax.ppermute(gram, 'rows', pairs[1])  2.53 us
    ppermute x1, starting transfers between devices, per_device(): lax.ppermute(gram, 'rows', pairs[0])  2.29 us
  transfers between devices with their start and end apart: 2, of which 2 were waited for; matrix products, arithmetic and copies ran while one was open for 0% of the time, Pallas kernels for 0%

profile of v1, /device:TPU:1, one launch (start us, length us, event | category | flops | bytes accessed | tf_op | source)
XLA Modules:
  0.0 78.5 jit_solution(12048783475511025055)
XLA Ops:
  1.3 0.0 copy-start.2
  1.9 0.0 copy-done.2
  2.0 0.0 copy-start
  2.0 0.7 copy-done
  2.7 0.0 copy-start.1
  2.7 0.7 copy-done.1
  3.4 43.8 %shard_map.68.samples_ref = f32[256,256]{1,0:T(8,128)S(1)} custom-call(f32[3,1024]{1,0:T(4,128)S(1)} %copy-done, bf16[3,128]{1,0:T(4,128)(2,1)S(1)} %copy-done.2, bf16[32,128]{1,0:T(8,128)(2,1)S(1)} %copy-done.1), custom_call_target="tpu_custom_call" | custom-call | tf_op jit(solution)/shard_map/pallas_call | solution.py:315
  47.2 8.2 %shard_map.69 = (f32[256,2,128]{2,1,0:T(2,128)}, f32[256,256]{1,0:T(8,128)S(1)}) custom-call(s32[1]{0:T(128)S(6)} %copy.7.size_ref, s32[1]{0:T(128)S(6)} %copy.8.rank_ref, f32[256,256]{1,0:T(8,128)S(1)} %shard_map.68.samples_ref), custom_call_target="tpu_custom_call" | custom-call | tf_op jit(solution)/shard_map/pallas_call | solution.py:341
  55.5 2.3 %collective-permute-start = (f32[256,256]{1,0:T(8,128)S(1)}, f32[256,256]{1,0:T(8,128)S(1)}, u32[]{:S(2)}, u32[]{:S(2)}) collective-permute-start(f32[256,256]{1,0:T(8,128)S(1)} %get-tuple-element.5.left_ref), channel_id=1, source_target_pairs={{0,8},{8,0},{16,24},{24,16},{32,40},{40,32},{48,56},{56,48},{64,72... | collective-permute-start | bytes 786440 | tf_op jit(solution)/shard_map/ppermute | solution.py:352
  57.8 1.1 %collective-permute-done.right_ref = f32[256,256]{1,0:T(8,128)S(1)} collective-permute-done((f32[256,256]{1,0:T(8,128)S(1)}, f32[256,256]{1,0:T(8,128)S(1)}, u32[]{:S(2)}, u32[]{:S(2)}) %collective-permute-start) | collective-permute-done | bytes 262176 | tf_op jit(solution)/shard_map/ppermute | solution.py:352
  58.9 2.6 %shard_map.70.left_ref = f32[256,256]{1,0:T(8,128)S(1)} custom-call(f32[256,256]{1,0:T(8,128)S(1)} %get-tuple-element.5.left_ref, f32[256,256]{1,0:T(8,128)S(1)} %collective-permute-done.right_ref), custom_call_target="tpu_custom_call" | custom-call | tf_op jit(solution)/shard_map/pallas_call | solution.py:350
  61.5 2.5 %collective-permute-start.1 = (f32[256,256]{1,0:T(8,128)S(1)}, f32[256,256]{1,0:T(8,128)S(1)}, u32[]{:S(2)}, u32[]{:S(2)}) collective-permute-start(f32[256,256]{1,0:T(8,128)S(1)} %shard_map.70.left_ref), channel_id=1, source_target_pairs={{0,16},{8,24},{16,0},{24,8},{32,48},{40,56},{48,32},{56,40},{64,80... | collective-permute-start | bytes 786440 | tf_op jit(solution)/shard_map/ppermute | solution.py:360
  64.0 6.9 %collective-permute-done.1.right_ref = f32[256,256]{1,0:T(8,128)S(1)} collective-permute-done((f32[256,256]{1,0:T(8,128)S(1)}, f32[256,256]{1,0:T(8,128)S(1)}, u32[]{:S(2)}, u32[]{:S(2)}) %collective-permute-start.1) | collective-permute-done | bytes 262176 | tf_op jit(solution)/shard_map/ppermute | solution.py:360
  70.9 7.6 %shard_map.71 = f32[1,256,256]{2,1,0:T(8,128)} custom-call(f32[256,256]{1,0:T(8,128)S(1)} %shard_map.70.left_ref, f32[256,256]{1,0:T(8,128)S(1)} %collective-permute-done.1.right_ref), custom_call_target="tpu_custom_call" | custom-call | tf_op jit(solution)/shard_map/pallas_call | solution.py:353
Async XLA Ops:
  1.3 0.7 copy-start.2
  2.0 0.7 copy-start
  2.7 0.7 copy-start.1
  55.5 3.4 %collective-permute-start = (f32[256,256]{1,0:T(8,128)S(1)}, f32[256,256]{1,0:T(8,128)S(1)}, u32[]{:S(2)}, u32[]{:S(2)}) collective-permute-start(f32[256,256]{1,0:T(8,128)S(1)} %get-tuple-element.5.left_ref), channel_id=1, source_target_pairs={{0,8},{8,0},{16,24},{24,16},{32,40},{40,32},{48,56},{56,48},{64,72... | collective-permute-start | bytes 786440 | tf_op jit(solution)/shard_map/ppermute | solution.py:352
  61.5 9.4 %collective-permute-start.1 = (f32[256,256]{1,0:T(8,128)S(1)}, f32[256,256]{1,0:T(8,128)S(1)}, u32[]{:S(2)}, u32[]{:S(2)}) collective-permute-start(f32[256,256]{1,0:T(8,128)S(1)} %shard_map.70.left_ref), channel_id=1, source_target_pairs={{0,16},{8,24},{16,0},{24,8},{32,48},{40,56},{48,32},{56,40},{64,80... | collective-permute-start | bytes 786440 | tf_op jit(solution)/shard_map/ppermute | solution.py:360

commit v2 on v1

--- a/solution.py
+++ b/solution.py
@@ -36,7 +36,7 @@
 
 def sample_kernel(
     col_total, targets_ref, sources_ref, probes_ref, out_ref,
-    tgt, src, spread, part_a, part_b, lhs, kmat, pair_out, own, pair_in, line_out, line_in,
+    tgt, src, spread, part_a, part_b, lhs, kmat, pair_out, own, pair_in, line_out, relay_in, line_in,
     send_sem, recv_sem,
 ):
     r, z = lax.axis_index("rows"), lax.axis_index("probe")
@@ -142,21 +142,33 @@
         lhs[: NPROBE // 2, cols] = part_a[yy].reshape(NPROBE // 2, LEAF)
         lhs[NPROBE // 2 :, cols] = part_b[:, yy].reshape(NPROBE // 2, LEAF)
     pair_copies, line_copies = [], []
-
-    def pass_on(group):
-        pair_copies[group].wait_recv()
-        line_out[group] = (own[group] + pair_in[group]).astype(line_out.dtype)
-        line_copies.append(send(line_out.at[group], line_in.at[group], xc_peer[(GROUPS[group], 0)]))
+    first, second = slice(0, NPROBE // 2), slice(NPROBE // 2, NPROBE)
+
+    def sums(group, rows):
+        return own[group, rows] + pair_in[group, rows]
+
+    def line(slot, rows, value, to_ref, dx):
+        line_out[slot, rows] = value
+        copy = send(line_out.at[slot, rows], to_ref.at[rows], xc_peer[(dx, 0)])
+        line_copies.append(copy)
+        return copy
 
     for group in range(len(GROUPS)):
         pair_copies.append(multiply(group))
-        if group >= 1:
-            pass_on(group - 1)
+    pair_copies[0].wait_recv()
+    relay = [line(0, first, sums(0, first), relay_in, 1), line(0, second, sums(0, second), relay_in, 3)]
+    pair_copies[1].wait_recv()
+    direct = [line(1, second, sums(1, second), line_in.at[0], 1)]
+    pair_copies[2].wait_recv()
+    direct.append(line(2, first, sums(2, first), line_in.at[1], 3))
+    relay[0].wait_recv()
+    direct.append(line(1, first, sums(1, first) + relay_in[first], line_in.at[0], 1))
+    relay[1].wait_recv()
+    direct.append(line(2, second, sums(2, second) + relay_in[second], line_in.at[1], 3))
     pair_copies[3].wait_recv()
-    total = own[3] + pair_in[3]
-    for group in range(3):
-        line_copies[group].wait_recv()
-        total = total + line_in[group].astype(F32)
+    for copy in direct:
+        copy.wait_recv()
+    total = (own[3] + pair_in[3]) + (line_in[0] + line_in[1])
     for half in range(2):
         for zz in range(NZ):
             to, frm = (2 * zz + half) * HALF, (half * NZ + zz) * HALF
@@ -246,7 +258,6 @@
 
 
 BASE = 32
-LINE = F32
 
 
 def chol_inverse(h, low, in_ref, out_ref):
@@ -277,7 +288,18 @@
     return jnp.sum(jnp.sum(kept, axis=0, keepdims=True), axis=1, keepdims=True) * (1.0 / NPROBE)
 
 
-def leaf_kernel(size_ref, rank_ref, samples_ref, basis_ref, gram_ref, in_ref, out_ref):
+def tree_kernel(
+    size_ref, rank_ref, samples_ref, basis_ref, top_ref,
+    in_ref, out_ref, gram_out, gram_in, node_out, node_in, send_sem, recv_sem,
+):
+    r, z = lax.axis_index("rows"), lax.axis_index("probe")
+    c, y = r % NC, (r // NC) % NY
+    sibling = (r + 1 - 2 * c, z)
+    cousin = (r + NC * (1 - 2 * (y % 2)), z)
+    barrier = pltpu.get_barrier_semaphore()
+    for peer in (sibling, cousin):
+        pl.semaphore_signal(barrier, inc=1, device_id=peer, device_id_type=MESH)
+
     col = lax.broadcasted_iota(jnp.int32, (NPROBE, 2 * LEAF), 1) % LEAF
     matrix = split(jnp.where(col < size_ref[0], samples_ref[...], 0.0))
     gram = dot_split(matrix, matrix, NT)
@@ -286,24 +308,43 @@
     row = lax.broadcasted_iota(jnp.int32, (NPROBE, NPROBE), 0)
     inverse = split(jnp.where(row < rank_ref[0], inverse, 0.0))
     projected = split(dot_split(inverse, split(gram)))
-    gram_ref[...] = dot_split(projected, projected, TN)
+    gram = dot_split(projected, projected, TN)
+    gram_out[...] = gram
+    pl.semaphore_wait(barrier, 2)
+
+    def send(from_ref, to_ref, slot, peer):
+        copy = pltpu.make_async_remote_copy(
+            src_ref=from_ref, dst_ref=to_ref, send_sem=send_sem.at[slot], recv_sem=recv_sem.at[slot],
+            device_id=peer, device_id_type=MESH,
+        )
+        copy.start()
+        return copy
+
+    pair = send(gram_out, gram_in, 0, sibling)
     basis = dot_split(inverse, matrix)
     basis_ref[:, 0, :] = basis[:, :LEAF]
     basis_ref[:, 1, :] = basis[:, LEAF:]
-
-
-def middle_kernel(left_ref, right_ref, gram_ref):
-    gram = left_ref[...] + right_ref[...]
+    pair.wait_recv()
+
+    gram = gram + gram_in[...]
     shift = shift_of(gram)
     inverse = spd_inverses([gram + shift * eye(NPROBE)], shift)[0]
-    gram_ref[...] = gram - shift * eye(NPROBE) + (shift * shift) * inverse
-
-
-def top_kernel(left_ref, right_ref, top_ref, in_ref, out_ref):
-    gram = left_ref[...] + right_ref[...]
+    gram = gram - shift * eye(NPROBE) + (shift * shift) * inverse
+    half = NPROBE // 2
+    node_out[0] = gram[:half, :half]
+    node_out[1] = gram[half:, :half]
+    node_out[2] = gram[half:, half:]
+    node = send(node_out, node_in, 1, cousin)
+    node.wait_recv()
+    part = [node_out[i] + node_in[i] for i in range(3)]
+    gram = jnp.concatenate(
+        [jnp.concatenate([part[0], part[1].T], axis=1), jnp.concatenate([part[1], part[2]], axis=1)], axis=0
+    )
     shift = shift_of(gram)
     inverse = chol_inverse(gram + shift * eye(NPROBE), shift, in_ref, out_ref)
     top_ref[0] = dot3(gram, inverse, NT)
+    pair.wait_send()
+    node.wait_send()
 
 
 def per_device(targets, sources, probes, cluster_sizes, leaf_ranks):
@@ -328,37 +369,36 @@
             pltpu.VMEM((4, NPROBE, 2 * LEAF), F32),
             pltpu.VMEM((4, NPROBE, 2 * LEAF), F32),
             pltpu.VMEM((4, NPROBE, 2 * LEAF), F32),
-            pltpu.VMEM((3, NPROBE, 2 * LEAF), LINE),
-            pltpu.VMEM((3, NPROBE, 2 * LEAF), LINE),
-            pltpu.SemaphoreType.DMA((49,)),
-            pltpu.SemaphoreType.DMA((49,)),
+            pltpu.VMEM((3, NPROBE, 2 * LEAF), F32),
+            pltpu.VMEM((NPROBE, 2 * LEAF), F32),
+            pltpu.VMEM((2, NPROBE, 2 * LEAF), F32),
+            pltpu.SemaphoreType.DMA((52,)),
+            pltpu.SemaphoreType.DMA((52,)),
         ],
         compiler_params=pltpu.CompilerParams(
             collective_id=0, has_side_effects=True, vmem_limit_bytes=40 * 1024 * 1024
         ),
     )(targets, sources, probes)
-    small = pltpu.CompilerParams(vmem_limit_bytes=40 * 1024 * 1024)
-    basis, gram = pl.pallas_call(
-        leaf_kernel,
-        out_shape=(jax.ShapeDtypeStruct((NPROBE, 2, LEAF), F32), square),
+    half = NPROBE // 2
+    return pl.pallas_call(
+        tree_kernel,
+        out_shape=(
+            jax.ShapeDtypeStruct((NPROBE, 2, LEAF), F32), jax.ShapeDtypeStruct((1, NPROBE, NPROBE), F32),
+        ),
         in_specs=[smem, smem, vmem],
         out_specs=(vmem, vmem),
-        scratch_shapes=base,
-        compiler_params=small,
+        scratch_shapes=base + [
+            pltpu.VMEM((NPROBE, NPROBE), F32),
+            pltpu.VMEM((NPROBE, NPROBE), F32),
+            pltpu.VMEM((3, half, half), F32),
+            pltpu.VMEM((3, half, half), F32),
+            pltpu.SemaphoreType.DMA((2,)),
+            pltpu.SemaphoreType.DMA((2,)),
+        ],
+        compiler_params=pltpu.CompilerParams(
+            collective_id=1, has_side_effects=True, vmem_limit_bytes=40 * 1024 * 1024
+        ),
     )(cluster_sizes, leaf_ranks, samples)
-    pairs = [[(s, s ^ bit) for s in range(lax.axis_size("rows"))] for bit in (1, 2)]
-    gram = pl.pallas_call(
-        middle_kernel, out_shape=square, in_specs=[vmem] * 2, out_specs=vmem, compiler_params=small
-    )(gram, lax.ppermute(gram, "rows", pairs[0]))
-    top = pl.pallas_call(
-        top_kernel,
-        out_shape=jax.ShapeDtypeStruct((1, NPROBE, NPROBE), F32),
-        in_specs=[vmem] * 2,
-        out_specs=vmem,
-        scratch_shapes=base,
-        compiler_params=small,
-    )(gram, lax.ppermute(gram, "rows", pairs[1]))
-    return basis, top
 
 
 def solution(mesh):

time: 78.9 us -> 72 us (0.913)
  waiting for transfers between devices: 8 us -> 0 us
  starting transfers between devices: 4.82 us -> 0 us
  Pallas kernels: 62.3 us -> 66.8 us
  local copies, waits for them, and re-layouts: 1.42 us -> 2.83 us
    ppermute x2 -> x0, waiting for transfers between devices: 8 us -> none  [the longest x1 6.86 us: per_device(): lax.ppermute(gram, 'rows', pairs[1])]
    pallas_call x3 -> x1, Pallas kernels: 18.4 us -> 25.7 us  [per_device(): pl.pallas_call(tree_kernel, out_shape=(jax.ShapeDtypeStruct((NPROBE, 2, L...]
    ppermute x2 -> x0, starting transfers between devices: 4.82 us -> none  [the longest x1 2.53 us: per_device(): lax.ppermute(gram, 'rows', pairs[1])]
    pallas_call x1, Pallas kernels: 43.8 us -> 41.1 us  [per_device(): pl.pallas_call(functools.partial(sample_kernel, col_total), out_shape=squ...]
    unnamed x6 -> x8, local copies, waits for them, and re-layouts: 1.42 us -> 2.83 us
  transfers between devices with their start and end apart: 2 -> 0, of which waited for: 2 -> 0; matrix products, arithmetic and copies ran while one was open for 0% -> 0% of each run, Pallas kernels for 0% -> 0%
where the time goes in v2:
time: 72 us; the launch traced here: 71.6 us
  Pallas kernels  66.8 us (93%)
  local copies, waits for them, and re-layouts  2.83 us (4%)
  between operations  1.97 us (3%)
    pallas_call x1, Pallas kernels, per_device(): pl.pallas_call(functools.partial(sample_kernel, col_total), out_shape=squ...  41.1 us
    pallas_call x1, Pallas kernels, per_device(): pl.pallas_call(tree_kernel, out_shape=(jax.ShapeDtypeStruct((NPROBE, 2, L...  25.7 us
    unnamed x8, local copies, waits for them, and re-layouts  2.83 us

profile of v2, /device:TPU:1, one launch (start us, length us, event | category | flops | bytes accessed | tf_op | source)
XLA Modules:
  0.0 71.6 jit_solution(8634300721683222678)
XLA Ops:
  1.3 0.0 copy-start.2
  1.9 0.0 copy-done.2
  2.0 0.0 copy-start
  2.0 0.7 copy-done
  2.7 0.0 copy-start.1
  2.7 0.7 copy-done.1
  3.4 41.1 %shard_map.68.samples_ref = f32[256,256]{1,0:T(8,128)S(1)} custom-call(f32[3,1024]{1,0:T(4,128)S(1)} %copy-done, bf16[3,128]{1,0:T(4,128)(2,1)S(1)} %copy-done.2, bf16[32,128]{1,0:T(8,128)(2,1)S(1)} %copy-done.1), custom_call_target="tpu_custom_call" | custom-call | tf_op jit(solution)/shard_map/pallas_call | solution.py:356
  44.5 25.7 %shard_map.69 = (f32[256,2,128]{2,1,0:T(2,128)S(1)}, f32[1,256,256]{2,1,0:T(8,128)S(1)}) custom-call(s32[1]{0:T(128)S(6)} %copy.9.size_ref, s32[1]{0:T(128)S(6)} %copy.10.rank_ref, f32[256,256]{1,0:T(8,128)S(1)} %shard_map.68.samples_ref), custom_call_target="tpu_custom_call" | custom-call | tf_op jit(solution)/shard_map/pallas_call | solution.py:383
  70.2 0.7 copy.11
  70.9 0.7 copy.12
Async XLA Ops:
  1.3 0.7 copy-start.2
  2.0 0.7 %copy-start = (f32[3,1024]{1,0:T(4,128)S(1)}, f32[3,1024]{1,0:T(4,128)}, u32[]{:S(2)}) copy-start(f32[3,1024]{1,0:T(4,128)} %targets_ref.1) | copy-start | bytes 36868
  2.7 0.7 copy-start.1
